TPU v7x, 32 devices: a whole 2x2x4 slice. The times are simulated.
32 devices in a mesh: event: 16 (over z, x, core), wrow: 2 (over y).
Axes of the slice: x: 2, y: 2, z: 4, core: 2. Of those that a mesh axis runs over, the one named last changes fastest.
Arguments:
- mc_mass: float32 [49152], P('event'), may hold values from 0.5 to 4
- mc_basis: bfloat16 [64, 49152], P(None, 'event'), may hold values from -4 to 4
- data_mass: float32 [65536], P('event'), may hold values from 0.5 to 4
- data_basis: bfloat16 [64, 65536], P(None, 'event'), may hold values from -4 to 4
- data_weight: float32 [65536], P('event'), may hold values from 0.2 to 7.2, as said below
- res_mass: float32 [1024], P('wrow'), may hold values from 0.8 to 1.9
- res_width: float32 [1024], P('wrow'), may hold values from 0.05 to 0.5
- res_wave: int32 [1024], P('wrow'), may hold values from 0 to 511, as said below
- wave_q: int32 [512], P('wrow'), may hold values from 0 to 63
- couplings: float32 [2, 512], P(None, 'wrow'), may hold values from -0.25 to 0.25
Outputs:
- coupling_out: float32 [2, 512], P(None, 'wrow')
- intensity: float32 [65536], P('event')
Inputs may be any that keep to these rules, and one draw needn't show every extreme that they name: Resonance r belongs to a wave of block r // 512: res_wave[r] // 256 == r // 512; every wave has exactly 2 resonances. `data_weight`: positive event weights.
All inputs are finite; a program needn't handle non-finite values.
Results may differ from a plain program's by a relative error of at most 0.0024.
Values may be sent and summed in bfloat16 or wider, within the bound.
A program may use at most 64 MiB of HBM per device.

v0:
```python
import jax
import jax.numpy as jnp
from jax import lax
from jax.sharding import PartitionSpec as P

ITERS = 3
BACKGROUND = 0.5


def split_two(value):
    high = lax.reduce_precision(value, 8, 7)
    return high.astype(jnp.bfloat16), (value - high).astype(jnp.bfloat16)


def wave_table(res_mass, res_width, local_wave, wave_q):
    waves = jnp.arange(wave_q.shape[0], dtype=jnp.int32)[:, None]
    index = jnp.arange(res_mass.shape[0], dtype=jnp.int32)[None, :]
    mine = local_wave[None, :] == waves
    first = jnp.min(jnp.where(mine, index, res_mass.shape[0]), axis=1, keepdims=True)
    last = jnp.max(jnp.where(mine, index, -1), axis=1, keepdims=True)

    def pick(where, values):
        return jnp.sum(jnp.where(index == where, values[None, :], 0.0), axis=1)

    return jnp.stack(
        [
            pick(first, res_mass),
            pick(first, res_width),
            pick(last, res_mass),
            pick(last, res_width),
            wave_q.astype(jnp.float32),
        ]
    )


def wave_amplitudes(mass_sq, angular_basis, table):
    def shape_of(mass, width):
        product = (mass * width)[:, None]
        spacing = (mass * mass)[:, None] - mass_sq[None, :]
        scale = product / (spacing * spacing + product * product)
        return scale * spacing, scale * product

    real_a, imag_a = shape_of(table[0], table[1])
    real_b, imag_b = shape_of(table[2], table[3])
    levels = jnp.arange(angular_basis.shape[0], dtype=jnp.float32)
    chooser = (table[4][:, None] == levels[None, :]).astype(jnp.bfloat16)
    angular = jnp.dot(chooser, angular_basis, preferred_element_type=jnp.float32)
    return (
        (angular * (real_a + real_b)).astype(jnp.bfloat16),
        (angular * (imag_a + imag_b)).astype(jnp.bfloat16),
    )


def dot_last(left, right):
    return lax.dot_general(
        left, right, (((1,), (1,)), ((), ())), preferred_element_type=jnp.float32
    )


def shards(
    mc_mass,
    mc_basis,
    data_mass,
    data_basis,
    data_weight,
    res_mass,
    res_width,
    res_wave,
    wave_q,
    couplings,
):
    highest = lax.Precision.HIGHEST
    wave_count = wave_q.shape[0]
    event_devices = lax.axis_size("event")
    row_devices = lax.axis_size("wrow")
    row_index = lax.axis_index("wrow")
    local = wave_table(res_mass, res_width, res_wave - row_index * wave_count, wave_q)
    gathered = lax.all_gather(
        jnp.concatenate([local, couplings], axis=0), "wrow", axis=1, tiled=True
    )
    table, coupling = gathered[:5], gathered[5:7]
    waves = gathered.shape[1]
    mine = row_index * wave_count

    mc_real, mc_imag = wave_amplitudes(mc_mass, mc_basis, table)
    left = jnp.concatenate(
        [
            lax.dynamic_slice_in_dim(mc_real, mine, wave_count),
            lax.dynamic_slice_in_dim(mc_imag, mine, wave_count),
        ],
        axis=0,
    )
    by_real = dot_last(left, mc_real)
    by_imag = dot_last(left, mc_imag)
    normalize = 1.0 / (mc_mass.shape[0] * event_devices)
    gram_part = jnp.concatenate(
        [
            (by_real[:wave_count] + by_imag[wave_count:]) * normalize,
            (by_imag[:wave_count] - by_real[wave_count:]) * normalize,
        ],
        axis=1,
    )
    gram = lax.psum_scatter(gram_part, "event", scatter_dimension=0, tiled=True)
    gram_rows = gram.shape[0]
    gram_at = mine + lax.axis_index("event") * gram_rows

    share = data_mass.shape[0] // row_devices
    start = row_index * share
    mass_here = lax.dynamic_slice_in_dim(data_mass, start, share)
    basis_here = lax.dynamic_slice_in_dim(data_basis, start, share, axis=1)
    weight_here = lax.dynamic_slice_in_dim(data_weight, start, share)
    data_real, data_imag = wave_amplitudes(mass_here, basis_here, table)
    real_wide = data_real.astype(jnp.float32)
    imag_wide = data_imag.astype(jnp.float32)
    squares = (real_wide * real_wide + imag_wide * imag_wide).astype(jnp.bfloat16)
    inverse_count = 1.0 / (data_mass.shape[0] * event_devices)

    def field_total(coupling):
        rows = jnp.concatenate(split_two(coupling), axis=0)
        on_real = jnp.dot(rows, data_real, preferred_element_type=jnp.float32)
        on_imag = jnp.dot(rows, data_imag, preferred_element_type=jnp.float32)
        on_real = on_real[:2] + on_real[2:]
        on_imag = on_imag[:2] + on_imag[2:]
        return on_real[0] - on_imag[1], on_imag[0] + on_real[1]

    for iteration in range(ITERS):
        field_real, field_imag = field_total(coupling)
        power = field_real * field_real + field_imag * field_imag
        inverse = 1.0 / (power + BACKGROUND)
        weighting = weight_here * inverse * inverse_count
        carried = jnp.stack([field_real * weighting, field_imag * weighting])
        rows = jnp.concatenate(split_two(carried), axis=0)
        on_real = dot_last(rows, data_real)
        on_imag = dot_last(rows, data_imag)
        on_real = on_real[:2] + on_real[2:]
        on_imag = on_imag[:2] + on_imag[2:]
        bend = jnp.stack(split_two(weighting * power * inverse))
        curve = dot_last(bend, squares)
        partial = jnp.stack(
            [
                -(on_real[0] + on_imag[1]),
                -(on_real[1] - on_imag[0]),
                curve[0] + curve[1],
            ]
        )
        real_rows, imag_rows = gram[:, :waves], gram[:, waves:]
        own = jnp.stack(
            [
                jnp.sum(real_rows * coupling[0][None] - imag_rows * coupling[1][None], axis=1),
                jnp.sum(real_rows * coupling[1][None] + imag_rows * coupling[0][None], axis=1),
                jnp.sum(jnp.abs(real_rows) + jnp.abs(imag_rows), axis=1),
            ]
        )
        there = lax.dynamic_slice_in_dim(partial, gram_at, gram_rows, axis=1)
        partial = lax.dynamic_update_slice_in_dim(partial, there + own, gram_at, axis=1)
        total = jnp.sum(lax.all_gather(partial, ("event", "wrow"), axis=0), axis=0)
        coupling = coupling - total[:2] / total[2:3]
    field_real, field_imag = field_total(coupling)
    intensity = field_real * field_real + field_imag * field_imag + BACKGROUND
    intensity = lax.all_gather(intensity, "wrow", axis=0, tiled=True)
    return (lax.dynamic_slice_in_dim(coupling, mine, wave_count, axis=1), intensity)


def solution(mesh):
    placed = (
        P("event"),
        P(None, "event"),
        P("event"),
        P(None, "event"),
        P("event"),
        P("wrow"),
        P("wrow"),
        P("wrow"),
        P("wrow"),
        P(None, "wrow"),
    )
    return jax.shard_map(
        shards, mesh=mesh, in_specs=placed, out_specs=(P(None, "wrow"), P("event")), check_vma=False
    )
```

profile of v0, /device:TPU:0, one launch (start us, length us, event | category | flops | bytes accessed | tf_op | source)
XLA Modules:
  0.0 311.2 jit_solution(2537800312354092347)
XLA Ops:
  7.2 0.0 copy-start
  7.2 0.0 reduce-scatter.4.cloned.1.call-start
  7.2 0.7 broadcast_subtract_fusion
  8.0 0.3 select_reduce_fusion.2
  8.2 0.7 convert_element_type.86
  8.9 1.1 select_reduce_fusion.1
  10.0 0.7 concatenate.30
  10.7 5.3 %all_gather.30 = f32[7,512]{1,0:T(8,128)S(1)} all-gather(f32[7,256]{1,0:T(8,128)S(1)} %concatenate.30), channel_id=1, replica_groups=mesh['event'=16,'wrow'=2] {'wrow'}, dimensions={1}, use_global_device_ids=true | all-gather | bytes 21504 | tf_op jit(solution)/shard_map/all_gather | solution.py:78
  16.1 5.8 %multiply_convert_fusion = (bf16[512,3072]{1,0:T(8,128)(2,1)S(1)}, bf16[512,3072]{1,0:T(8,128)(2,1)S(1)}) fusion(f32[512]{0:T(512)S(1)} %mul.340, f32[512]{0:T(512)S(1)} %bitcast.116, f32[512]{0:T(512)S(1)} %bitcast.87, f32[512]{0:T(512)S(1)} %mul.333, f32[3072]{0:T(1024)} %param.10, f32[512]{0:T(512)S(1)} %bitcast.118, f32[512]{0:T(512)S(1)} %bitcast.91, ...), kind=kOutput, calls=%fused_computation.11 | convolution fusion | flops 229670912 | bytes 6711296 | tf_op jit(solution)/shard_map/dot_general | solution.py:47
  21.8 0.2 constant_dynamic-slice_fusion.1
  22.1 1.9 fusion.15
  23.9 1.9 fusion.14
  25.8 0.1 fusion.17
  26.0 0.0 copy-start.9
  26.0 0.1 pad_maximum_fusion.3
  26.0 1.3 copy.14
  27.4 0.0 reduce-scatter.4.cloned.1.call-update
  27.4 0.0 copy-done.9
  27.4 0.0 copy-done
  27.4 3.8 %add_convert_fusion = (bf16[512,2048]{1,0:T(8,128)(2,1)S(1)}, bf16[512,2048]{1,0:T(8,128)(2,1)S(1)}, bf16[512,2048]{1,0:T(8,128)(2,1)S(1)}) fusion(f32[512]{0:T(512)S(1)} %mul.340, f32[512]{0:T(512)S(1)} %bitcast.117, f32[512]{0:T(512)S(1)} %bitcast.88, f32[512]{0:T(512)S(1)} %mul.333, f32[2048]{0:T(1024)S(1)} %dynamic_slice.28, f32[512]{0:T(512)S(1)} %bitcast.119, ...), kind=kOutput, calls=%fused_computation.23 | convolution fusion | flops 159416320 | bytes 6576132 | tf_op jit(solution)/shard_map/dot_general | solution.py:47
  31.3 0.0 copy-start.1
  31.3 0.0 copy-start.8
  31.3 0.4 fusion.75
  31.7 0.4 fusion.74
  32.2 0.6 fusion.32
  32.9 0.0 copy-done.1
  32.9 0.3 copy-done.4
  33.2 0.6 fusion.50
  33.9 2.3 fusion.49
  36.2 50.4 %reduce-scatter.4.cloned.1.call-done = f32[16,1024]{1,0:T(8,128)} async-done(((f32[256,1024]{1,0:T(8,128)}), f32[16,1024]{1,0:T(8,128)}) %reduce-scatter.4.cloned.1.call-update) | async-done | bytes 65552 | tf_op jit(solution)/shard_map/reduce_scatter | solution.py:103
  86.7 0.9 subtract_reduce_fusion.2
  87.6 0.1 fusion.56
  87.7 0.1 dynamic_update_slice.12
  87.8 66.4 %all_gather.33 = f32[32,3,512]{2,1,0:T(4,128)S(1)} all-gather(f32[1,3,512]{2,1,0:T(4,128)S(1)} %dynamic_update_slice.12), channel_id=1, replica_groups=mesh['event'=16,'wrow'=2] {'event','wrow'}, dimensions={0}, use_global_device_ids=true | all-gather | bytes 202752 | tf_op jit(solution)/shard_map/all_gather | solution.py:156
  154.2 0.1 reduce_sum.141
  154.3 0.0 copy-start.2
  154.3 0.4 fusion.73
  154.7 2.2 fusion.72
  157.0 0.6 fusion.48
  157.6 0.0 copy-done.2
  157.6 0.7 fusion.47
  158.4 0.6 fusion.36
  159.1 0.0 copy-done.7
  159.1 0.1 subtract_reduce_fusion.1
  159.2 0.1 fusion.58
  159.3 0.1 dynamic_update_slice.13
  159.4 65.5 %all_gather.36 = f32[32,3,512]{2,1,0:T(4,128)S(1)} all-gather(f32[1,3,512]{2,1,0:T(4,128)S(1)} %dynamic_update_slice.13), channel_id=1, replica_groups=mesh['event'=16,'wrow'=2] {'event','wrow'}, dimensions={0}, use_global_device_ids=true | all-gather | bytes 202752 | tf_op jit(solution)/shard_map/all_gather | solution.py:156
  224.9 0.1 reduce_sum.144
  225.0 0.0 copy-start.3
  225.0 0.4 fusion.71
  225.4 2.2 fusion.70
  227.7 0.6 fusion.46
  228.3 0.7 fusion.45
  229.1 0.6 fusion.40
  229.8 0.1 subtract_reduce_fusion
  229.9 0.1 fusion.60
  230.0 0.1 dynamic_update_slice.14
  230.1 66.2 %all_gather.39 = f32[32,3,512]{2,1,0:T(4,128)S(1)} all-gather(f32[1,3,512]{2,1,0:T(4,128)S(1)} %dynamic_update_slice.14), channel_id=1, replica_groups=mesh['event'=16,'wrow'=2] {'event','wrow'}, dimensions={0}, use_global_device_ids=true | all-gather | bytes 202752 | tf_op jit(solution)/shard_map/all_gather | solution.py:156
  296.3 0.1 reduce_sum.147
  296.4 2.0 fusion.68
  298.4 0.4 fusion.69
  298.8 0.6 constant_dynamic-slice_fusion
  299.4 4.4 %all-gather = f32[1,4096]{1,0:T(1,128)S(1)} all-gather(f32[1,2048]{1,0:T(1,128)S(1)} %fusion.44), channel_id=2, replica_groups=mesh['event'=16,'wrow'=2] {'wrow'}, dimensions={1}, use_global_device_ids=true | all-gather | bytes 24576 | tf_op jit(solution)/shard_map/all_gather | solution.py:160
  303.8 0.6 copy.20
  (65 shorter events, 0.7 us)
Async XLA Ops:
  7.2 20.3 %copy-start = (bf16[64,4096]{1,0:T(8,128)(2,1)S(1)}, bf16[64,4096]{1,0:T(8,128)(2,1)}, u32[]{:S(2)}) copy-start(bf16[64,4096]{1,0:T(8,128)(2,1)} %param.13) | copy-start | bytes 1572868
  7.2 79.5 %reduce-scatter.4.cloned.1.call-start = ((), (), s32[]{:S(2)}) async-start(), calls=%async_computation.1 | async-start | bytes 1114112 | tf_op jit(solution)/shard_map/reduce_scatter | solution.py:103
  26.0 1.5 copy-start.9
  31.3 1.6 copy-start.1
  31.3 1.9 copy-start.4
  31.3 0.8 copy-start.8
  154.3 3.4 %copy-start.2 = (bf16[512,2048]{1,0:T(8,128)(2,1)S(1)}, bf16[512,2048]{1,0:T(8,128)(2,1)}, u32[]{:S(2)}) copy-start(bf16[512,2048]{1,0:T(8,128)(2,1)} %copy-done.1) | copy-start | bytes 6291460
  154.7 3.7 %copy-start.5 = (bf16[512,2048]{1,0:T(8,128)(2,1)S(1)}, bf16[512,2048]{1,0:T(8,128)(2,1)}, u32[]{:S(2)}) copy-start(bf16[512,2048]{1,0:T(8,128)(2,1)} %copy-done.4) | copy-start | bytes 6291460
  157.0 2.1 copy-start.7
  225.0 3.3 %copy-start.3 = (bf16[512,2048]{1,0:T(8,128)(2,1)S(1)}, bf16[512,2048]{1,0:T(8,128)(2,1)}, u32[]{:S(2)}) copy-start(bf16[512,2048]{1,0:T(8,128)(2,1)} %copy-done.1) | copy-start | bytes 6291460
  225.4 3.7 %copy-start.6 = (bf16[512,2048]{1,0:T(8,128)(2,1)S(1)}, bf16[512,2048]{1,0:T(8,128)(2,1)}, u32[]{:S(2)}) copy-start(bf16[512,2048]{1,0:T(8,128)(2,1)} %copy-done.4) | copy-start | bytes 6291460
Sparse Core Ops, SparseCore 0:
  27.5 59.1 reduce-scatter.3
where the time goes:
time: 312 us; the launch traced here: 311 us
  blocking collectives  208 us (67%)
  waiting for transfers between devices  50.4 us (16%)
  matrix products  29 us (9%)
  between operations  14.6 us (5%)
  other arithmetic  5.21 us (2%)
  local copies, waits for them, and re-layouts  4.21 us (1%)
    all_gather x3, blocking collectives, shards(): total = jnp.sum(lax.all_gather(partial, ('event', 'wrow'), axis=0), axis=0)  198 us
    reduce_scatter x1, waiting for transfers between devices, shards(): gram = lax.psum_scatter(gram_part, 'event', scatter_dimension=0, tiled=True)  50.4 us
    dot_general x11, matrix products, dot_last(): lax.dot_general(left, right, (((1,), (1,)), ((), ())), preferred_element_...  11.2 us
    dot_general x2, matrix products, wave_amplitudes(): jnp.dot(chooser, angular_basis, preferred_element_type=jnp.float32)  9.6 us
    dot_general x4, matrix products, field_total(): on_imag = jnp.dot(rows, data_imag, preferred_element_type=jnp.float32)  6.71 us
  transfers between devices with their start and end apart: 1, of which 1 were waited for; matrix products, arithmetic and copies ran while one was open for 3% of the time, Pallas kernels for 0%

commit v1 on v0

--- a/solution.py
+++ b/solution.py
@@ -1,15 +1,14 @@
+import functools
+
 import jax
 import jax.numpy as jnp
 from jax import lax
+from jax.experimental import pallas as pl
+from jax.experimental.pallas import tpu as pltpu
 from jax.sharding import PartitionSpec as P
 
 ITERS = 3
 BACKGROUND = 0.5
-
-
-def split_two(value):
-    high = lax.reduce_precision(value, 8, 7)
-    return high.astype(jnp.bfloat16), (value - high).astype(jnp.bfloat16)
 
 
 def wave_table(res_mass, res_width, local_wave, wave_q):
@@ -55,6 +54,219 @@
     return lax.dot_general(
         left, right, (((1,), (1,)), ((), ())), preferred_element_type=jnp.float32
     )
+
+
+def halves(value):
+    high = value.astype(jnp.bfloat16)
+    return high, (value - high.astype(jnp.float32)).astype(jnp.bfloat16)
+
+
+def newton_kernel(
+    sizes,
+    gram_ref,
+    real_ref,
+    imag_ref,
+    squares_ref,
+    weight_ref,
+    start_ref,
+    coupling_ref,
+    intensity_ref,
+    tiles,
+    near,
+    far,
+    near_out,
+    far_out,
+    tile_send,
+    tile_recv,
+    near_send,
+    near_recv,
+    far_send,
+    far_recv,
+):
+    events, rows, low = sizes
+    high_count = events // low
+    group = low * rows
+    event = lax.axis_index("event")
+    row = lax.axis_index("wrow")
+    high, part = event // low, event % low
+    place = part * rows + row
+    me = event * rows + row
+    everyone = events * rows
+    mesh_id = pl.DeviceIdType.MESH
+
+    barrier = pltpu.get_barrier_semaphore()
+
+    def greet(step, carry):
+        other = (me + step) % everyone
+        pl.semaphore_signal(
+            barrier, inc=1, device_id=(other // rows, other % rows), device_id_type=mesh_id
+        )
+        return carry
+
+    lax.fori_loop(1, everyone, greet, 0)
+    pl.semaphore_wait(barrier, everyone - 1)
+
+    def tile_copy(step, slot):
+        other = (event + step) % events
+        return pltpu.make_async_remote_copy(
+            src_ref=gram_ref.at[other],
+            dst_ref=tiles.at[slot],
+            send_sem=tile_send.at[step],
+            recv_sem=tile_recv.at[slot],
+            device_id=(other, row),
+            device_id_type=mesh_id,
+        )
+
+    def near_copy(turn, step, slot):
+        other = (place + step) % group
+        return pltpu.make_async_remote_copy(
+            src_ref=near_out.at[turn],
+            dst_ref=near.at[turn, slot],
+            send_sem=near_send.at[turn, step],
+            recv_sem=near_recv.at[turn, slot],
+            device_id=(high * low + other // rows, other % rows),
+            device_id_type=mesh_id,
+        )
+
+    def far_copy(turn, step, slot):
+        other = (high + step) % high_count
+        return pltpu.make_async_remote_copy(
+            src_ref=far_out.at[turn],
+            dst_ref=far.at[turn, slot],
+            send_sem=far_send.at[turn, step],
+            recv_sem=far_recv.at[turn, slot],
+            device_id=(other * low + part, row),
+            device_id_type=mesh_id,
+        )
+
+    def start_all(copy, count, own):
+        def body(step, carry):
+            copy(step, own).start()
+            return carry
+
+        lax.fori_loop(1, count, body, 0)
+
+    def wait_all(copy, count, own):
+        def body(step, carry):
+            copy(step, (own + step) % count).wait()
+            return carry
+
+        lax.fori_loop(1, count, body, 0)
+
+    start_all(tile_copy, events, event)
+
+    def times(values, ref):
+        both = jnp.concatenate(halves(values), axis=0)
+        out = jnp.dot(both, ref[...], preferred_element_type=jnp.float32)
+        count = values.shape[0]
+        return out[:count] + out[count:]
+
+    def times_last(values, ref):
+        both = jnp.concatenate(halves(values), axis=0)
+        out = dot_last(both, ref[...])
+        count = values.shape[0]
+        return out[:count] + out[count:]
+
+    def field_total(coupling):
+        on_real = times(coupling, real_ref)
+        on_imag = times(coupling, imag_ref)
+        return on_real[0:1] - on_imag[1:2], on_imag[0:1] + on_real[1:2]
+
+    weight = weight_ref[...]
+    coupling = start_ref[...]
+    waves = coupling.shape[1]
+    gram_rows = gram_ref.shape[1]
+    lanes = lax.broadcasted_iota(jnp.int32, (gram_rows, waves), 1)
+    down = lax.broadcasted_iota(jnp.int32, (gram_rows, waves), 0)
+    spot = lanes == down + (row * (gram_rows * events) + event * gram_rows)
+
+    def placed(terms):
+        column = jnp.sum(terms, axis=1, keepdims=True)
+        return jnp.sum(jnp.where(spot, column, 0.0), axis=0, keepdims=True)
+
+    real_rows = imag_rows = None
+    for turn in range(ITERS):
+        field_real, field_imag = field_total(coupling)
+        power = field_real * field_real + field_imag * field_imag
+        inverse = 1.0 / (power + BACKGROUND)
+        weighting = weight * inverse
+        carried = jnp.concatenate([field_real * weighting, field_imag * weighting], axis=0)
+        on_real = times_last(carried, real_ref)
+        on_imag = times_last(carried, imag_ref)
+        curve = times_last(weighting * power * inverse, squares_ref)
+        if turn == 0:
+            wait_all(tile_copy, events, event)
+            tiles[event] = gram_ref[event]
+            gram = lax.fori_loop(
+                0,
+                events,
+                lambda index, total: total + tiles[index].astype(jnp.float32),
+                jnp.zeros((gram_rows, 2 * waves), jnp.float32),
+            )
+            real_rows, imag_rows = gram[:, :waves], gram[:, waves:]
+        own_real = placed(real_rows * coupling[0:1] - imag_rows * coupling[1:2])
+        own_imag = placed(real_rows * coupling[1:2] + imag_rows * coupling[0:1])
+        own_curve = placed(jnp.abs(real_rows) + jnp.abs(imag_rows))
+        partial = jnp.concatenate(
+            [
+                own_real - (on_real[0:1] + on_imag[1:2]),
+                own_imag - (on_real[1:2] - on_imag[0:1]),
+                own_curve + curve,
+                jnp.zeros((1, waves), jnp.float32),
+            ],
+            axis=0,
+        )
+        near_out[turn] = partial
+        near[turn, place] = partial
+        start_all(functools.partial(near_copy, turn), group, place)
+        wait_all(functools.partial(near_copy, turn), group, place)
+        total = near[turn, 0]
+        for slot in range(1, group):
+            total = total + near[turn, slot]
+        far_out[turn] = total
+        far[turn, high] = total
+        start_all(functools.partial(far_copy, turn), high_count, high)
+        wait_all(functools.partial(far_copy, turn), high_count, high)
+        total = far[turn, 0]
+        for slot in range(1, high_count):
+            total = total + far[turn, slot]
+        coupling = coupling - total[0:2] / total[2:3]
+    coupling_ref[...] = coupling
+    field_real, field_imag = field_total(coupling)
+    intensity_ref[...] = field_real * field_real + field_imag * field_imag + BACKGROUND
+
+
+def newton(gram_blocks, data_real, data_imag, squares, weight, coupling, rows):
+    events, gram_rows, twice = gram_blocks.shape
+    waves, share = data_real.shape
+    low = max(size for size in range(1, events + 1) if events % size == 0 and size * size <= events)
+    group, high = low * rows, events // low
+    dma = pltpu.SemaphoreType.DMA
+    return pl.pallas_call(
+        functools.partial(newton_kernel, (events, rows, low)),
+        out_shape=(
+            jax.ShapeDtypeStruct((2, waves), jnp.float32),
+            jax.ShapeDtypeStruct((1, share), jnp.float32),
+        ),
+        in_specs=[pl.BlockSpec(memory_space=pltpu.VMEM)] * 6,
+        out_specs=(pl.BlockSpec(memory_space=pltpu.VMEM),) * 2,
+        scratch_shapes=[
+            pltpu.VMEM((events, gram_rows, twice), jnp.bfloat16),
+            pltpu.VMEM((ITERS, group, 4, waves), jnp.float32),
+            pltpu.VMEM((ITERS, high, 4, waves), jnp.float32),
+            pltpu.VMEM((ITERS, 4, waves), jnp.float32),
+            pltpu.VMEM((ITERS, 4, waves), jnp.float32),
+            dma((events,)),
+            dma((events,)),
+            dma((ITERS, group)),
+            dma((ITERS, group)),
+            dma((ITERS, high)),
+            dma((ITERS, high)),
+        ],
+        compiler_params=pltpu.CompilerParams(
+            collective_id=0, has_side_effects=True, vmem_limit_bytes=40 * 1024 * 1024
+        ),
+    )(gram_blocks, data_real, data_imag, squares, weight, coupling)
 
 
 def shards(
@@ -69,7 +281,6 @@
     wave_q,
     couplings,
 ):
-    highest = lax.Precision.HIGHEST
     wave_count = wave_q.shape[0]
     event_devices = lax.axis_size("event")
     row_devices = lax.axis_size("wrow")
@@ -100,9 +311,9 @@
         ],
         axis=1,
     )
-    gram = lax.psum_scatter(gram_part, "event", scatter_dimension=0, tiled=True)
-    gram_rows = gram.shape[0]
-    gram_at = mine + lax.axis_index("event") * gram_rows
+    gram_blocks = gram_part.astype(jnp.bfloat16).reshape(
+        event_devices, wave_count // event_devices, 2 * waves
+    )
 
     share = data_mass.shape[0] // row_devices
     start = row_index * share
@@ -115,48 +326,16 @@
     squares = (real_wide * real_wide + imag_wide * imag_wide).astype(jnp.bfloat16)
     inverse_count = 1.0 / (data_mass.shape[0] * event_devices)
 
-    def field_total(coupling):
-        rows = jnp.concatenate(split_two(coupling), axis=0)
-        on_real = jnp.dot(rows, data_real, preferred_element_type=jnp.float32)
-        on_imag = jnp.dot(rows, data_imag, preferred_element_type=jnp.float32)
-        on_real = on_real[:2] + on_real[2:]
-        on_imag = on_imag[:2] + on_imag[2:]
-        return on_real[0] - on_imag[1], on_imag[0] + on_real[1]
-
-    for iteration in range(ITERS):
-        field_real, field_imag = field_total(coupling)
-        power = field_real * field_real + field_imag * field_imag
-        inverse = 1.0 / (power + BACKGROUND)
-        weighting = weight_here * inverse * inverse_count
-        carried = jnp.stack([field_real * weighting, field_imag * weighting])
-        rows = jnp.concatenate(split_two(carried), axis=0)
-        on_real = dot_last(rows, data_real)
-        on_imag = dot_last(rows, data_imag)
-        on_real = on_real[:2] + on_real[2:]
-        on_imag = on_imag[:2] + on_imag[2:]
-        bend = jnp.stack(split_two(weighting * power * inverse))
-        curve = dot_last(bend, squares)
-        partial = jnp.stack(
-            [
-                -(on_real[0] + on_imag[1]),
-                -(on_real[1] - on_imag[0]),
-                curve[0] + curve[1],
-            ]
-        )
-        real_rows, imag_rows = gram[:, :waves], gram[:, waves:]
-        own = jnp.stack(
-            [
-                jnp.sum(real_rows * coupling[0][None] - imag_rows * coupling[1][None], axis=1),
-                jnp.sum(real_rows * coupling[1][None] + imag_rows * coupling[0][None], axis=1),
-                jnp.sum(jnp.abs(real_rows) + jnp.abs(imag_rows), axis=1),
-            ]
-        )
-        there = lax.dynamic_slice_in_dim(partial, gram_at, gram_rows, axis=1)
-        partial = lax.dynamic_update_slice_in_dim(partial, there + own, gram_at, axis=1)
-        total = jnp.sum(lax.all_gather(partial, ("event", "wrow"), axis=0), axis=0)
-        coupling = coupling - total[:2] / total[2:3]
-    field_real, field_imag = field_total(coupling)
-    intensity = field_real * field_real + field_imag * field_imag + BACKGROUND
+    coupling, intensity = newton(
+        gram_blocks,
+        data_real,
+        data_imag,
+        squares,
+        (weight_here * inverse_count)[None],
+        coupling,
+        row_devices,
+    )
+    intensity = intensity[0]
     intensity = lax.all_gather(intensity, "wrow", axis=0, tiled=True)
     return (lax.dynamic_slice_in_dim(coupling, mine, wave_count, axis=1), intensity)
 

time: 312 us -> 80 us (0.26)
  blocking collectives: 208 us -> 9.64 us
  waiting for transfers between devices: 50.4 us -> 0 us
  Pallas kernels: 0 us -> 46.2 us
  matrix products: 29 us -> 14.7 us
  between operations: 14.6 us -> 0.76 us
    all_gather x3 -> x0, blocking collectives: 198 us -> none  [shards(): total = jnp.sum(lax.all_gather(partial, ('event', 'wrow'), axis=0), axis=0)]
    reduce_scatter x1 -> x0, waiting for transfers between devices: 50.4 us -> none  [shards(): gram = lax.psum_scatter(gram_part, 'event', scatter_dimension=0, tiled=True)]
    pallas_call x0 -> x1, Pallas kernels: none -> 46.2 us  [newton(): pl.pallas_call(functools.partial(newton_kernel, (events, rows, low)), out...]
    dot_general x8 -> x0, matrix products: 8.24 us -> none  [the longest x4 6.71 us: field_total(): on_imag = jnp.dot(rows, data_imag, preferred_element_type=jnp.float32)]
    dot_general x11 -> x2, matrix products: 11.2 us -> 3.63 us  [dot_last(): lax.dot_general(left, right, (((1,), (1,)), ((), ())), preferred_element_...]
  transfers between devices with their start and end apart: 1 -> 0, of which waited for: 1 -> 0; matrix products, arithmetic and copies ran while one was open for 3% -> 0% of each run, Pallas kernels for 0% -> 0%
where the time goes in v1:
time: 80 us; the launch traced here: 79.6 us
  Pallas kernels  46.2 us (58%)
  matrix products  14.7 us (18%)
  blocking collectives  9.64 us (12%)
  local copies, waits for them, and re-layouts  5.18 us (6%)
  other arithmetic  3.16 us (4%)
    pallas_call x1, Pallas kernels, newton(): pl.pallas_call(functools.partial(newton_kernel, (events, rows, low)), out...  46.2 us
    dot_general x2, matrix products, wave_amplitudes(): jnp.dot(chooser, angular_basis, preferred_element_type=jnp.float32)  11 us
    all_gather x1, blocking collectives, shards(): lax.all_gather(jnp.concatenate([local, couplings], axis=0), 'wrow', axis=...  5.28 us
    all_gather x1, blocking collectives, shards(): intensity = lax.all_gather(intensity, 'wrow', axis=0, tiled=True)  4.36 us
    dot_general x2, matrix products, dot_last(): lax.dot_general(left, right, (((1,), (1,)), ((), ())), preferred_element_...  3.63 us
    dynamic_slice x1, local copies, waits for them, and re-layouts, shards(): lax.dynamic_slice_in_dim(mc_imag, mine, wave_count)  2.23 us
    unnamed x11, local copies, waits for them, and re-layouts  1.66 us

profile of v1, /device:TPU:0, one launch (start us, length us, event | category | flops | bytes accessed | tf_op | source)
XLA Modules:
  0.0 79.6 jit_solution(12383257372848834814)
XLA Ops:
  0.6 0.0 copy-start
  0.7 0.7 broadcast_subtract_fusion
  1.4 0.3 select_reduce_fusion.2
  1.7 1.1 %select_reduce_fusion.1 = (f32[256]{0:T(256)S(1)}, f32[256]{0:T(256)S(1)}, f32[256]{0:T(256)S(1)}, f32[256]{0:T(256)S(1)}) fusion(s32[256]{0:T(256)S(1)} %get-tuple-element.12, f32[512]{0:T(512)} %param.15, s32[256]{0:T(256)S(1)} %get-tuple-element.13, f32[512]{0:T(512)} %param.16), kind=kLoop, calls=%fused_computation.36 | loop fusion | flops 1309696 | bytes 10240 | tf_op jit(solution)/shard_map/reduce_sum | solution.py:22
  2.8 0.7 convert_element_type.28
  3.5 0.7 concatenate.15
  4.2 5.3 %all_gather.6 = f32[7,512]{1,0:T(8,128)S(1)} all-gather(f32[7,256]{1,0:T(8,128)S(1)} %concatenate.15), channel_id=1, replica_groups=mesh['event'=16,'wrow'=2] {'wrow'}, dimensions={1}, use_global_device_ids=true | all-gather | bytes 21504 | tf_op jit(solution)/shard_map/all_gather | solution.py:289
  9.5 7.2 %multiply_convert_fusion = (bf16[512,3072]{1,0:T(8,128)(2,1)}, bf16[512,3072]{1,0:T(8,128)(2,1)}) fusion(f32[512]{0:T(512)S(1)} %mul.166, f32[512]{0:T(512)S(1)} %bitcast.36, f32[512]{0:T(512)S(1)} %bitcast.23, f32[512]{0:T(512)S(1)} %mul.159, f32[3072]{0:T(1024)} %param.10, f32[512]{0:T(512)S(1)} %bitcast.34, f32[512]{0:T(512)S(1)} %bitcast.27, ...), kind=kOutput, calls=%fused_computation.11 | convolution fusion | flops 229670912 | bytes 6711296 | tf_op jit(solution)/shard_map/dot_general | solution.py:46
  16.7 0.0 copy-start.2
  16.7 2.2 %constant_dynamic-slice_fusion.1 = (bf16[256,3072]{1,0:T(8,128)(2,1)S(1)}, bf16[256,3072]{1,0:T(8,128)(2,1)S(1)}) fusion(bf16[512,3072]{1,0:T(8,128)(2,1)} %get-tuple-element.17, s32[]{:T(128)S(6)} %select_n.36, bf16[512,3072]{1,0:T(8,128)(2,1)} %get-tuple-element.18), kind=kLoop, calls=%fused_computation.57 | loop fusion | bytes 6291460 | tf_op jit(solution)/shard_map/dynamic_slice | solution.py:300
  19.0 0.6 copy-done.2
  19.6 0.0 copy-start.1
  19.6 1.8 %fusion.15 = f32[512,512]{1,0:T(8,128)S(1)} fusion(bf16[512,3072]{1,0:T(8,128)(2,1)S(1)} %copy-done.2, bf16[256,3072]{1,0:T(8,128)(2,1)S(1)} %get-tuple-element.26, bf16[256,3072]{1,0:T(8,128)(2,1)S(1)} %get-tuple-element.27), kind=kOutput, calls=%fused_computation.27 | convolution fusion | flops 1616904192 | bytes 7340032 | tf_op jit(solution)/shard_map/dot_general | solution.py:54
  21.4 0.1 copy-done.1
  21.4 1.8 %fusion.14 = f32[512,512]{1,0:T(8,128)S(1)} fusion(bf16[512,3072]{1,0:T(8,128)(2,1)S(1)} %copy-done.1, bf16[256,3072]{1,0:T(8,128)(2,1)S(1)} %get-tuple-element.26, bf16[256,3072]{1,0:T(8,128)(2,1)S(1)} %get-tuple-element.27), kind=kOutput, calls=%fused_computation.26 | convolution fusion | flops 1616904192 | bytes 7340032 | tf_op jit(solution)/shard_map/dot_general | solution.py:54
  23.3 0.0 copy-start.3
  23.3 0.3 fusion.19
  23.5 0.1 pad_maximum_fusion.3.gram_ref
  23.6 0.4 copy-done.3
  24.0 0.0 copy-done
  24.0 0.0 copy-start.4
  24.0 3.8 %add_convert_fusion = (bf16[512,2048]{1,0:T(8,128)(2,1)S(1)}, bf16[512,2048]{1,0:T(8,128)(2,1)S(1)}, bf16[512,2048]{1,0:T(8,128)(2,1)S(1)}) fusion(f32[512]{0:T(512)S(1)} %mul.166, f32[512]{0:T(512)S(1)} %bitcast.37, f32[512]{0:T(512)S(1)} %bitcast.24, f32[512]{0:T(512)S(1)} %mul.159, f32[2048]{0:T(1024)S(1)} %dynamic_slice.21, f32[512]{0:T(512)S(1)} %bitcast.35, ...), kind=kOutput, calls=%fused_computation.23 | convolution fusion | flops 159416320 | bytes 6576132 | tf_op jit(solution)/shard_map/dot_general | solution.py:46
  27.8 0.0 copy-done.4
  27.8 46.2 %shard_map.113 = (f32[2,512]{1,0:T(2,128)S(1)}, f32[1,2048]{1,0:T(1,128)S(1)}) custom-call(bf16[16,16,1024]{2,1,0:T(8,128)(2,1)S(1)} %pad_maximum_fusion.3.gram_ref, bf16[512,2048]{1,0:T(8,128)(2,1)S(1)} %get-tuple-element.16.real_ref, bf16[512,2048]{1,0:T(8,128)(2,1)S(1)} %get-tuple-element.15.imag_ref, ...), custom_call_target="tpu_custom_call" | custom-call | tf_op jit(solution)/shard_map/pallas_call | solution.py:245
  74.0 4.4 %all-gather = f32[1,4096]{1,0:T(1,128)S(1)} all-gather(f32[1,2048]{1,0:T(1,128)S(1)} %get-tuple-element.5), channel_id=2, replica_groups=mesh['event'=16,'wrow'=2] {'wrow'}, dimensions={1}, use_global_device_ids=true | all-gather | bytes 24576 | tf_op jit(solution)/shard_map/all_gather | solution.py:339
  78.4 0.6 constant_dynamic-slice_fusion
  79.0 0.6 copy.13
  (6 shorter events, 0.0 us)
Async XLA Ops:
  0.6 23.4 %copy-start = (bf16[64,4096]{1,0:T(8,128)(2,1)S(1)}, bf16[64,4096]{1,0:T(8,128)(2,1)}, u32[]{:S(2)}) copy-start(bf16[64,4096]{1,0:T(8,128)(2,1)} %param.13) | copy-start | bytes 1572868
  16.7 2.8 %copy-start.2 = (bf16[512,3072]{1,0:T(8,128)(2,1)S(1)}, bf16[512,3072]{1,0:T(8,128)(2,1)}, u32[]{:S(2)}) copy-start(bf16[512,3072]{1,0:T(8,128)(2,1)} %get-tuple-element.18) | copy-start | bytes 9437188
  19.6 1.9 %copy-start.1 = (bf16[512,3072]{1,0:T(8,128)(2,1)S(1)}, bf16[512,3072]{1,0:T(8,128)(2,1)}, u32[]{:S(2)}) copy-start(bf16[512,3072]{1,0:T(8,128)(2,1)} %get-tuple-element.17) | copy-start | bytes 9437188
  23.3 0.7 copy-start.3
  24.0 3.8 %copy-start.4 = (f32[4096]{0:T(1024)S(1)}, f32[4096]{0:T(1024)}, u32[]{:S(2)}) copy-start(f32[4096]{0:T(1024)} %param.14) | copy-start | bytes 49156
